TPU v7x, 32 devices: a whole 2x2x4 slice. The times are simulated.
32 devices in a mesh: seq: 16 (over z, y, x), piece: 2 (over core).
Axes of the slice: x: 2, y: 2, z: 4, core: 2. Of those that a mesh axis runs over, the one named last changes fastest.
Arguments:
- query: bfloat16 [2048, 2048], P('seq', 'piece'), may hold values from -64 to 64
- key_rows: bfloat16 [2048, 2048], P('seq', 'piece'), may hold values from -64 to 64
- value_matrix_rows: bfloat16 [2048, 2048], P('seq', 'piece'), may hold values from -6 to 6
- grad_out: bfloat16 [2048, 2048], P('seq', 'piece'), may hold values from -6 to 6
- rel_embed: bfloat16 [512, 64], replicated, may hold values from -6 to 6
Outputs:
- grad_query: bfloat16 [2048, 2048], P('seq', 'piece')
- grad_key: bfloat16 [2048, 2048], P('seq', 'piece')
- grad_value: bfloat16 [2048, 2048], P('seq', 'piece')
- grad_embed: float32 [512, 64], replicated
All inputs are finite; a program needn't handle non-finite values.
Results may differ from a plain program's by a relative error of at most 0.0086.
Values may be sent and summed in bfloat16 or wider, within the bound.
A program may use at most 64 MiB of HBM per device.

v0:
```python
import functools

import jax
import jax.numpy as jnp
from jax import lax
from jax.experimental import pallas as pl
from jax.experimental.pallas import tpu as pltpu
from jax.sharding import PartitionSpec as P

HEAD_DIM = 64
BAND_EXTENT = 512
LANES = 128
MESH = pl.DeviceIdType.MESH
NT = (((1,), (1,)), ((), ()))
NEG = float("-inf")


def dot(left, right, dims=(((1,), (0,)), ((), ()))):
    return lax.dot_general(left, right, dims, preferred_element_type=jnp.float32)


def skew(along):
    return pltpu.roll(along, 1, 1, stride=1, stride_axis=0)


def mirror(size):
    down = lax.broadcasted_iota(jnp.int32, (size, size), 0)
    across = lax.broadcasted_iota(jnp.int32, (size, size), 1)
    return (down + across == size - 1).astype(jnp.float32).astype(jnp.bfloat16)


def reverse_columns(value, flips):
    parts, stop = [], value.shape[1]
    wide = flips.shape[0]
    while stop:
        size = stop % wide or wide
        parts.append(dot(value[:, stop - size : stop], flips[wide - size :, :size]))
        stop -= size
    return jnp.concatenate(parts, axis=1)


def band_kernel(
    seq_count, piece_count, group, pairs,
    q_ref, k_ref, v_ref, do_ref, emb_ref,
    gq_ref, gk_ref, gv_ref, ge_ref,
    qg, dg, kg, vg, ql, kl, vl, sq, sk, sv, dkt, dvt, det, ee, en,
    de_own, l1, s2, l2, s3, de_all,
    in_s, in_r, h_s, h_r, q_s, q_r, own_s, own_r, back_s, back_r, e1_s, e1_r, e2_s, e2_r, e3_s, e3_r,
):
    rows = q_ref.shape[0]
    band = group * rows
    window = band + rows
    groups = seq_count // group
    mates = group * piece_count
    feat = HEAD_DIM // mates
    seq, piece = lax.axis_index("seq"), lax.axis_index("piece")
    mine, member = seq // group, seq % group
    place = member * piece_count + piece
    has_prev, has_next = mine > 0, mine < groups - 1

    def at(which, index, core):
        return (which * group + index, core)

    def mate(step):
        other = lax.rem(place + step, mates)
        return other, at(mine, other // piece_count, lax.rem(other, piece_count))

    barrier = pltpu.get_barrier_semaphore()

    def greet(device):
        pl.semaphore_signal(barrier, inc=1, device_id=device, device_id_type=MESH)

    for step in range(1, mates):
        greet(mate(step)[1])
    for step in range(1, groups):
        greet(at(lax.rem(mine + step, groups), member, piece))

    @pl.when(has_prev)
    def _():
        for step in range(1, group):
            greet(at(mine - 1, lax.rem(member + step, group), piece))

    @pl.when(has_next)
    def _():
        for step in range(1, group):
            greet(at(mine + 1, lax.rem(member + step, group), piece))

    sides = jnp.where(has_prev, 1, 0) + jnp.where(has_next, 1, 0)
    pl.semaphore_wait(barrier, mates - 1 + groups - 1 + (group - 1) * sides)

    def cols(owner, pair):
        return pl.ds(pl.multiple_of((owner * pairs + pair) * LANES, LANES), LANES)

    def block(index):
        return pl.ds(pl.multiple_of(index * rows, rows), rows)

    def spread(kind, pair, step):
        source = (k_ref, v_ref, q_ref, do_ref)[kind]
        target = (kg, vg, qg, dg)[kind]
        base = (group, group, 0, 0)[kind]
        to = lax.rem(member + step, group)
        return pltpu.make_async_remote_copy(
            src_ref=source.at[:, cols(to, pair)],
            dst_ref=target.at[pair, block(base + member)],
            send_sem=in_s.at[kind, pair, step], recv_sem=in_r.at[kind, pair, step],
            device_id=at(mine, to, piece), device_id_type=MESH,
        )

    def forward(kind, pair, index):
        target = (kg, vg)[kind]
        return pltpu.make_async_remote_copy(
            src_ref=target.at[pair, block(group + index)],
            dst_ref=target.at[pair, block(index)],
            send_sem=h_s.at[kind, pair, index], recv_sem=h_r.at[kind, pair, index],
            device_id=at(mine + 1, member, piece), device_id_type=MESH,
        )

    def to_query_owner(pair, index):
        return pltpu.make_async_remote_copy(
            src_ref=sq.at[pair, index], dst_ref=ql.at[member, pair],
            send_sem=q_s.at[pair, index], recv_sem=q_r.at[pair, member],
            device_id=at(mine, index, piece), device_id_type=MESH,
        )

    def to_key_owner(kind, pair, index):
        return pltpu.make_async_remote_copy(
            src_ref=(sk, sv)[kind].at[pair, group + index], dst_ref=(kl, vl)[kind].at[0, member, pair],
            send_sem=own_s.at[kind, pair, index], recv_sem=own_r.at[kind, pair, member],
            device_id=at(mine, index, piece), device_id_type=MESH,
        )

    def to_earlier_owner(kind, pair, index):
        return pltpu.make_async_remote_copy(
            src_ref=(sk, sv)[kind].at[pair, index], dst_ref=(kl, vl)[kind].at[1, member, pair],
            send_sem=back_s.at[kind, pair, index], recv_sem=back_r.at[kind, pair, member],
            device_id=at(mine - 1, index, piece), device_id_type=MESH,
        )

    def landed(target, sem):
        pltpu.make_async_copy(target, target, sem).wait()

    order = ((0, 1), (2, 3))
    for kinds in order:
        for pair in range(pairs):
            for step in range(1, group):
                for kind in kinds:
                    spread(kind, pair, step).start()
            for kind in kinds:
                source = (k_ref, v_ref, q_ref, do_ref)[kind]
                base = (group, group, 0, 0)[kind]
                (kg, vg, qg, dg)[kind][pair, block(base + member), :] = source[:, cols(member, pair)]
            if kinds == (0, 1):

                @pl.when(has_next)
                def _(pair=pair):
                    for kind in (0, 1):
                        forward(kind, pair, member).start()

    @pl.when(jnp.logical_not(has_prev))
    def _():
        for pair in range(pairs):
            kg[pair, :band, :] = jnp.zeros((band, LANES), kg.dtype)
            vg[pair, :band, :] = jnp.zeros((band, LANES), vg.dtype)

    flips = mirror(2 * rows)
    flip = flips[rows:, :rows]
    feature = lax.broadcasted_iota(jnp.int32, (HEAD_DIM, LANES), 0)
    twice = (lax.rem(lax.broadcasted_iota(jnp.int32, (HEAD_DIM, LANES), 1), HEAD_DIM) == feature).astype(jnp.float32)
    for index in range(group):
        turned = dot(flip, emb_ref[(group - 1 - index) * rows : (group - index) * rows, :])
        ee[index * rows : (index + 1) * rows, :] = dot(
            turned.astype(jnp.bfloat16), twice.astype(jnp.bfloat16)
        ).astype(jnp.bfloat16)
    en[...] = dot(emb_ref[...], twice.astype(jnp.bfloat16)).astype(jnp.bfloat16)
    det[...] = jnp.zeros_like(det)

    for pair in range(pairs):
        for step in range(1, group):
            for kind in (0, 1):
                spread(kind, pair, step).wait_recv()

            @pl.when(has_next)
            def _(pair=pair, step=step):
                for kind in (0, 1):
                    forward(kind, pair, lax.rem(member + group - step, group)).start()

    scale = HEAD_DIM ** (-0.5)
    lane = lax.broadcasted_iota(jnp.int32, (1, LANES), 1)
    low = (lane < HEAD_DIM).astype(jnp.float32)
    high = 1.0 - low

    def halves(value, factor):
        return jnp.concatenate(
            [value * (low * factor).astype(jnp.bfloat16), value * (high * factor).astype(jnp.bfloat16)], axis=0
        )

    for pair in range(pairs):
        for step in range(1, group):
            for kind in (2, 3):
                spread(kind, pair, step).wait_recv()

        @pl.when(has_prev)
        def _(pair=pair):
            for index in range(group):
                for kind in (0, 1):
                    forward(kind, pair, index).wait_recv()

        dkt[...] = jnp.zeros_like(dkt)
        dvt[...] = jnp.zeros_like(dvt)

        def step_block(index, carry, pair=pair):
            start = pl.multiple_of(index * rows, rows)
            span = pl.ds(start, window)
            q2 = halves(qg[pair, pl.ds(start, rows), :], scale)
            do2 = halves(dg[pair, pl.ds(start, rows), :], 1.0)
            keys, vals = kg[pair, span, :], vg[pair, span, :]
            emb = ee[...]
            along = dot(q2, emb, NT)
            along = jnp.concatenate([along, jnp.full((2 * rows, rows), NEG, jnp.float32)], axis=1)
            along = jnp.concatenate([skew(along[:rows]), skew(along[rows:])], axis=0)
            column = lax.broadcasted_iota(jnp.int32, (1, window), 1) + start + jnp.where(has_prev, band, 0)
            absent = jnp.where(column < band, NEG, 0.0)
            score = dot(q2, keys, NT) + along + absent
            top = jnp.max(score, axis=1, keepdims=True)
            expd = jnp.exp(score - top)
            prob = expd * (1.0 / jnp.sum(expd, axis=1, keepdims=True))
            prob_b = prob.astype(jnp.bfloat16)
            dprob = dot(do2, vals, NT)
            delta = jnp.sum(prob_b.astype(jnp.float32) * dprob, axis=1, keepdims=True)
            dscore = prob * (dprob - delta)
            dscore_b = dscore.astype(jnp.bfloat16)
            dalong = reverse_columns(dscore_b, flips)
            dalong = jnp.concatenate([skew(dalong[:rows]), skew(dalong[rows:])], axis=0)
            dalong_b = dalong[:, rows:].astype(jnp.bfloat16)
            gq2 = dot(dscore_b, keys) + dot(dalong_b, en[...])
            gq = gq2[:rows] * (low * scale) + gq2[rows:] * (high * scale)
            sq[pair, index] = gq.astype(jnp.bfloat16)
            q2t, do2t = q2.T, do2.T
            dkt[:, span] += dot(q2t, dscore_b)
            dvt[:, span] += dot(do2t, prob_b)
            det[...] += dot(q2t, dalong_b)

            @pl.when(index != member)
            def _():
                to_query_owner(pair, index).start()

            @pl.when(has_prev)
            def _():
                sk[pair, index] = dkt[:, pl.ds(start, rows)].T.astype(jnp.bfloat16)
                sv[pair, index] = dvt[:, pl.ds(start, rows)].T.astype(jnp.bfloat16)
                for kind in (0, 1):
                    to_earlier_owner(kind, pair, index).start()

            return carry

        lax.fori_loop(0, group, step_block, 0)

        if pair == pairs - 1:
            de_own[...] = det[:HEAD_DIM, :] + det[HEAD_DIM:, :]
            for step in range(1, mates):
                share(mate, place, mates, feat, step, de_own, l1, e1_s, e1_r).start()

        def hand_over(index, carry, pair=pair):
            near = pl.ds(pl.multiple_of(band + index * rows, rows), rows)
            sk[pair, group + index] = dkt[:, near].T.astype(jnp.bfloat16)
            sv[pair, group + index] = dvt[:, near].T.astype(jnp.bfloat16)

            @pl.when(index != member)
            def _():
                for kind in (0, 1):
                    to_key_owner(kind, pair, index).start()

            return carry

        lax.fori_loop(0, group, hand_over, 0)
        ql[member, pair] = sq[pair, member]
        kl[0, member, pair] = sk[pair, group + member]
        vl[0, member, pair] = sv[pair, group + member]

    own_rows = pl.ds(pl.multiple_of(place * feat, feat), feat)
    l1[place] = de_own[own_rows, :]
    for step in range(1, mates):
        share(mate, place, mates, feat, step, de_own, l1, e1_s, e1_r).wait_recv()
    total = l1[0]
    for index in range(1, mates):
        total = total + l1[index]
    s2[...] = total
    l2[mine] = total

    def across(step):
        return pltpu.make_async_remote_copy(
            src_ref=s2, dst_ref=l2.at[mine], send_sem=e2_s.at[step], recv_sem=e2_r.at[step],
            device_id=at(lax.rem(mine + step, groups), member, piece), device_id_type=MESH,
        )

    def give(step):
        return pltpu.make_async_remote_copy(
            src_ref=s3, dst_ref=de_all.at[own_rows], send_sem=e3_s.at[step], recv_sem=e3_r.at[step],
            device_id=mate(step)[1], device_id_type=MESH,
        )

    for step in range(1, groups):
        across(step).start()

    for pair in range(pairs):
        for step in range(1, group):
            source = lax.rem(member + step, group)
            landed(ql.at[source, pair], q_r.at[pair, source])
        for index in range(group):
            gq_ref[:, (index * pairs + pair) * LANES : (index * pairs + pair + 1) * LANES] = ql[index, pair]

    for step in range(1, groups):
        across(step).wait_recv()
    total = l2[0]
    for index in range(1, groups):
        total = total + l2[index]
    s3[...] = total
    de_all[own_rows, :] = total
    for step in range(1, mates):
        give(step).start()

    for pair in range(pairs):
        for step in range(1, group):
            source = lax.rem(member + step, group)
            for kind in (0, 1):
                landed((kl, vl)[kind].at[0, source, pair], own_r.at[kind, pair, source])

        @pl.when(has_next)
        def _(pair=pair):
            for source in range(group):
                for kind in (0, 1):
                    landed((kl, vl)[kind].at[1, source, pair], back_r.at[kind, pair, source])

        @pl.when(jnp.logical_not(has_next))
        def _(pair=pair):
            for source in range(group):
                for land in (kl, vl):
                    land[1, source, pair] = jnp.zeros((rows, LANES), land.dtype)

        for index in range(group):
            spot = slice((index * pairs + pair) * LANES, (index * pairs + pair + 1) * LANES)
            for land, out in ((kl, gk_ref), (vl, gv_ref)):
                out[:, spot] = (
                    land[0, index, pair].astype(jnp.float32) + land[1, index, pair].astype(jnp.float32)
                ).astype(jnp.bfloat16)

    for step in range(1, mates):
        give(step).wait_recv()
    ge_ref[...] = de_all[...].T

    for pair in range(pairs):
        for step in range(1, group):
            for kind in range(4):
                spread(kind, pair, step).wait_send()
        for index in range(group):

            @pl.when(has_next)
            def _(pair=pair, index=index):
                for kind in (0, 1):
                    forward(kind, pair, index).wait_send()

            @pl.when(has_prev)
            def _(pair=pair, index=index):
                for kind in (0, 1):
                    to_earlier_owner(kind, pair, index).wait_send()

            @pl.when(index != member)
            def _(pair=pair, index=index):
                to_query_owner(pair, index).wait_send()
                for kind in (0, 1):
                    to_key_owner(kind, pair, index).wait_send()

    for step in range(1, mates):
        share(mate, place, mates, feat, step, de_own, l1, e1_s, e1_r).wait_send()
        give(step).wait_send()
    for step in range(1, groups):
        across(step).wait_send()


def share(mate, place, mates, feat, step, de_own, l1, e1_s, e1_r):
    other, device = mate(step)
    return pltpu.make_async_remote_copy(
        src_ref=de_own.at[pl.ds(pl.multiple_of(other * feat, feat), feat)],
        dst_ref=l1.at[place],
        send_sem=e1_s.at[step], recv_sem=e1_r.at[step],
        device_id=device, device_id_type=MESH,
    )


def grouped(seq_count, piece_count, query, key_rows, value_matrix_rows, grad_out, rel_embed):
    rows, width = query.shape
    group = BAND_EXTENT // rows
    pairs = width // (group * LANES)
    groups, mates = seq_count // group, group * piece_count
    feat = HEAD_DIM // mates
    b16, f32 = jnp.bfloat16, jnp.float32
    vmem, dma = pltpu.VMEM, pltpu.SemaphoreType.DMA
    out = jax.ShapeDtypeStruct((rows, width), b16)
    whole = pl.BlockSpec(memory_space=pltpu.VMEM)
    return pl.pallas_call(
        functools.partial(band_kernel, seq_count, piece_count, group, pairs),
        out_shape=(out, out, out, jax.ShapeDtypeStruct((BAND_EXTENT, HEAD_DIM), f32)),
        in_specs=[whole] * 5,
        out_specs=(whole,) * 4,
        scratch_shapes=[
            vmem((pairs, group * rows, LANES), b16), vmem((pairs, group * rows, LANES), b16),
            vmem((pairs, 2 * group * rows, LANES), b16), vmem((pairs, 2 * group * rows, LANES), b16),
            vmem((group, pairs, rows, LANES), b16),
            vmem((2, group, pairs, rows, LANES), b16), vmem((2, group, pairs, rows, LANES), b16),
            vmem((pairs, group, rows, LANES), b16),
            vmem((pairs, 2 * group, rows, LANES), b16), vmem((pairs, 2 * group, rows, LANES), b16),
            vmem((LANES, 2 * group * rows), f32), vmem((LANES, 2 * group * rows), f32),
            vmem((LANES, BAND_EXTENT), f32), vmem((BAND_EXTENT, LANES), b16), vmem((BAND_EXTENT, LANES), b16),
            vmem((HEAD_DIM, BAND_EXTENT), f32), vmem((mates, feat, BAND_EXTENT), f32),
            vmem((feat, BAND_EXTENT), f32), vmem((groups, feat, BAND_EXTENT), f32),
            vmem((feat, BAND_EXTENT), f32), vmem((HEAD_DIM, BAND_EXTENT), f32),
            dma((4, pairs, group)), dma((4, pairs, group)),
            dma((2, pairs, group)), dma((2, pairs, group)),
            dma((pairs, group)), dma((pairs, group)),
            dma((2, pairs, group)), dma((2, pairs, group)),
            dma((2, pairs, group)), dma((2, pairs, group)),
            dma((mates,)), dma((mates,)), dma((groups,)), dma((groups,)), dma((mates,)), dma((mates,)),
        ],
        compiler_params=pltpu.CompilerParams(
            collective_id=0, has_side_effects=True, vmem_limit_bytes=40 * 2**20
        ),
    )(query, key_rows, value_matrix_rows, grad_out, rel_embed)


def shifted(value, axis, steps):
    count = lax.axis_size(axis)
    leading, last = (max(0, -steps), min(count, count - steps))
    return lax.ppermute(value, axis, [(source, source + steps) for source in range(leading, last)])


def skew_rel(along):
    head_count, row_tiles, cols = along.shape
    padded = jnp.pad(along, ((0, 0), (0, 0), (0, row_tiles)))
    flat = padded.reshape(head_count, row_tiles * (cols + row_tiles))[
        :, : row_tiles * (cols + row_tiles - 1)
    ]
    return flat.reshape(head_count, row_tiles, cols + row_tiles - 1)[
        :, :, row_tiles : 2 * row_tiles
    ]


def unskew_rel(dscore, cols):
    zeros = jnp.zeros(dscore.shape[:2] + (cols,), dscore.dtype)
    _, pull = jax.vjp(skew_rel, zeros)
    return pull(dscore)[0]


def embed_slice(emb_pad, offset, row_tiles):
    return emb_pad[offset + 1 : offset + 2 * row_tiles + 1][::-1]


def masked_scores(query, keys, slab, offset, present, scale):
    row_tiles = query.shape[0]
    direct = jnp.einsum("thd,shd->hts", query, keys, preferred_element_type=jnp.float32)
    along = jnp.einsum("thd,rd->htr", query, slab, preferred_element_type=jnp.float32)
    score = scale * (direct + skew_rel(along))
    qpos = lax.broadcasted_iota(jnp.int32, (row_tiles, row_tiles), 0)
    kpos = lax.broadcasted_iota(jnp.int32, (row_tiles, row_tiles), 1)
    dist = offset + qpos - kpos
    valid = (dist >= 0) & (dist < BAND_EXTENT) & present
    return jnp.where(valid[None], score, -jnp.inf)


def pair_grads(prob, query, value_tensor, dout, delta, scale):
    prob_b = prob.astype(jnp.bfloat16)
    dprob = jnp.einsum("thd,shd->hts", dout, value_tensor, preferred_element_type=jnp.float32)
    dscore = (prob * (dprob - delta[:, :, None]) * scale).astype(jnp.bfloat16)
    gkey = jnp.einsum("hts,thd->shd", dscore, query, preferred_element_type=jnp.float32)
    gvalue = jnp.einsum("hts,thd->shd", prob_b, dout, preferred_element_type=jnp.float32)
    return (dscore, gkey, gvalue)


def query_terms(dscore, keys, slab, query):
    dalong = unskew_rel(dscore, slab.shape[0])
    gquery = jnp.einsum("hts,shd->thd", dscore, keys, preferred_element_type=jnp.float32)
    gquery = gquery + jnp.einsum("htr,rd->thd", dalong, slab, preferred_element_type=jnp.float32)
    gembed = jnp.einsum("htr,thd->rd", dalong, query, preferred_element_type=jnp.float32)
    return (gquery, gembed)


def local(query, key_rows, value_matrix_rows, grad_out, rel_embed):
    row_tiles = query.shape[0]
    width = query.shape[1]
    head_feature_width = HEAD_DIM
    head_count = width // head_feature_width
    scale = head_feature_width ** (-0.5)
    reach = BAND_EXTENT // row_tiles
    here = lax.axis_index("seq")
    qh = query.reshape(row_tiles, head_count, head_feature_width)
    kh = key_rows.reshape(row_tiles, head_count, head_feature_width)
    vh = value_matrix_rows.reshape(row_tiles, head_count, head_feature_width)
    doh = grad_out.reshape(row_tiles, head_count, head_feature_width)
    emb_pad = jnp.pad(rel_embed, ((row_tiles, row_tiles + 1), (0, 0)))
    slabs = [embed_slice(emb_pad, step * row_tiles, row_tiles) for step in range(reach + 1)]
    windows = [(kh, vh)]
    for step in range(1, reach + 1):
        windows.append(shifted((kh, vh), "seq", step))
    scores = [
        masked_scores(qh, windows[step][0], slabs[step], step * row_tiles, here >= step, scale)
        for step in range(reach + 1)
    ]
    top = scores[0].max(axis=2)
    for score in scores[1:]:
        top = jnp.maximum(top, score.max(axis=2))
    total = jnp.zeros_like(top)
    for score in scores:
        total = total + jnp.exp(score - top[:, :, None]).sum(axis=2)
    lse = top + jnp.log(total)
    probs = [jnp.exp(score - lse[:, :, None]) for score in scores]
    attn_out = jnp.zeros((row_tiles, head_count, head_feature_width), jnp.float32)
    for step in range(reach + 1):
        attn_out = attn_out + jnp.einsum(
            "hts,shd->thd",
            probs[step].astype(jnp.bfloat16),
            windows[step][1],
            preferred_element_type=jnp.float32,
        )
    delta = jnp.sum(doh.astype(jnp.float32) * attn_out, axis=2).T
    grad_q = jnp.zeros((row_tiles, head_count, head_feature_width), jnp.float32)
    emb_grad = jnp.zeros(emb_pad.shape, jnp.float32)
    key_parts = []
    value_parts = []
    for step in range(reach + 1):
        dscore, gkey, gvalue = pair_grads(probs[step], qh, windows[step][1], doh, delta, scale)
        gquery, gembed = query_terms(dscore, windows[step][0], slabs[step], qh)
        grad_q = grad_q + gquery
        offset = step * row_tiles
        emb_grad = emb_grad.at[offset + 1 : offset + 2 * row_tiles + 1].add(gembed[::-1])
        key_parts.append(gkey)
        value_parts.append(gvalue)
    grad_k = key_parts[0]
    grad_v = value_parts[0]
    for step in range(1, reach + 1):
        back_k, back_v = shifted((key_parts[step], value_parts[step]), "seq", -step)
        grad_k = grad_k + back_k
        grad_v = grad_v + back_v
    local_embed = emb_grad[row_tiles : row_tiles + BAND_EXTENT]
    grad_embed = lax.psum(local_embed, ("seq", "piece"))
    grad_query = grad_q.reshape(row_tiles, width).astype(jnp.bfloat16)
    grad_key = grad_k.reshape(row_tiles, width).astype(jnp.bfloat16)
    grad_value = grad_v.reshape(row_tiles, width).astype(jnp.bfloat16)
    return (grad_query, grad_key, grad_value, grad_embed)


def solution(mesh):
    placed = (P("seq", "piece"), P("seq", "piece"), P("seq", "piece"), P("seq", "piece"), P())
    seq_count, piece_count = mesh.shape["seq"], mesh.shape["piece"]

    def body(query, key_rows, value_matrix_rows, grad_out, rel_embed):
        rows, width = query.shape
        group = BAND_EXTENT // rows
        mates = group * piece_count
        if rows == LANES and seq_count % group == 0 and width % (group * LANES) == 0 and HEAD_DIM % (8 * mates) == 0:
            return grouped(seq_count, piece_count, query, key_rows, value_matrix_rows, grad_out, rel_embed)
        return local(query, key_rows, value_matrix_rows, grad_out, rel_embed)

    return jax.shard_map(
        body,
        mesh=mesh,
        in_specs=placed,
        out_specs=(P("seq", "piece"), P("seq", "piece"), P("seq", "piece"), P()),
        check_vma=False,
    )
```

profile of v0, /device:TPU:0, one launch (start us, length us, event | category | flops | bytes accessed | tf_op | source)
XLA Modules:
  0.0 53.3 jit_solution(9811417338114501531)
XLA Ops:
  0.6 1.0 %copy.9.emb_ref = bf16[512,64]{1,0:T(8,128)(2,1)S(1)} copy(bf16[512,64]{0,1:T(8,128)(2,1)} %param.9) | data formatting | bytes 131072 | tf_op args[4]
  1.6 0.0 copy-start
  1.6 0.9 %copy-done = bf16[128,1024]{1,0:T(8,128)(2,1)S(1)} copy-done((bf16[128,1024]{1,0:T(8,128)(2,1)S(1)}, bf16[128,1024]{1,0:T(8,128)(2,1)}, u32[]{:S(2)}) %copy-start) | copy-done | bytes 262168
  2.5 0.0 copy-start.1
  2.6 0.9 %copy-done.1 = bf16[128,1024]{1,0:T(8,128)(2,1)S(1)} copy-done((bf16[128,1024]{1,0:T(8,128)(2,1)S(1)}, bf16[128,1024]{1,0:T(8,128)(2,1)}, u32[]{:S(2)}) %copy-start.1) | copy-done | bytes 262168
  3.5 0.0 copy-start.2
  3.5 0.9 %copy-done.2 = bf16[128,1024]{1,0:T(8,128)(2,1)S(1)} copy-done((bf16[128,1024]{1,0:T(8,128)(2,1)S(1)}, bf16[128,1024]{1,0:T(8,128)(2,1)}, u32[]{:S(2)}) %copy-start.2) | copy-done | bytes 262168
  4.5 0.0 copy-start.3
  4.5 0.9 %copy-done.3 = bf16[128,1024]{1,0:T(8,128)(2,1)S(1)} copy-done((bf16[128,1024]{1,0:T(8,128)(2,1)S(1)}, bf16[128,1024]{1,0:T(8,128)(2,1)}, u32[]{:S(2)}) %copy-start.3) | copy-done | bytes 262168
  5.4 45.0 %shard_map.84 = (bf16[128,1024]{1,0:T(8,128)(2,1)S(1)}, bf16[128,1024]{1,0:T(8,128)(2,1)S(1)}, bf16[128,1024]{1,0:T(8,128)(2,1)S(1)}, f32[512,64]{1,0:T(8,128)S(1)}) custom-call(bf16[128,1024]{1,0:T(8,128)(2,1)S(1)} %copy-done, bf16[128,1024]{1,0:T(8,128)(2,1)S(1)} %copy-done.1, bf16[128,1024]{1,0:T(8,128)(2,1)S(1)} %copy-done.2, ...), custom_call_target="tpu_custom_call" | custom-call | tf_op jit(solution)/shard_map/pallas_call | solution.py:400
  50.4 0.8 %copy.10 = f32[512,64]{0,1:T(8,128)} copy(f32[512,64]{1,0:T(8,128)S(1)} %get-tuple-element.7) | data formatting | bytes 262144 | tf_op jit(solution)/shard_map/pallas_call | solution.py:400
  51.1 0.7 %copy.14 = bf16[128,1024]{1,0:T(8,128)(2,1)} copy(bf16[128,1024]{1,0:T(8,128)(2,1)S(1)} %get-tuple-element.12) | data formatting | bytes 524288
  51.9 0.7 %copy.15 = bf16[128,1024]{1,0:T(8,128)(2,1)} copy(bf16[128,1024]{1,0:T(8,128)(2,1)S(1)} %get-tuple-element.13) | data formatting | bytes 524288
  52.6 0.7 %copy.16 = bf16[128,1024]{1,0:T(8,128)(2,1)} copy(bf16[128,1024]{1,0:T(8,128)(2,1)S(1)} %get-tuple-element.14) | data formatting | bytes 524288
Async XLA Ops:
  1.6 1.0 %copy-start = (bf16[128,1024]{1,0:T(8,128)(2,1)S(1)}, bf16[128,1024]{1,0:T(8,128)(2,1)}, u32[]{:S(2)}) copy-start(bf16[128,1024]{1,0:T(8,128)(2,1)} %q_ref.1) | copy-start | bytes 786436
  2.5 0.9 %copy-start.1 = (bf16[128,1024]{1,0:T(8,128)(2,1)S(1)}, bf16[128,1024]{1,0:T(8,128)(2,1)}, u32[]{:S(2)}) copy-start(bf16[128,1024]{1,0:T(8,128)(2,1)} %k_ref.1) | copy-start | bytes 786436
  3.5 0.9 %copy-start.2 = (bf16[128,1024]{1,0:T(8,128)(2,1)S(1)}, bf16[128,1024]{1,0:T(8,128)(2,1)}, u32[]{:S(2)}) copy-start(bf16[128,1024]{1,0:T(8,128)(2,1)} %v_ref.1) | copy-start | bytes 786436
  4.5 0.9 %copy-start.3 = (bf16[128,1024]{1,0:T(8,128)(2,1)S(1)}, bf16[128,1024]{1,0:T(8,128)(2,1)}, u32[]{:S(2)}) copy-start(bf16[128,1024]{1,0:T(8,128)(2,1)} %do_ref.1) | copy-start | bytes 786436
where the time goes:
time: 53.5 us; the launch traced here: 53.3 us
  Pallas kernels  45 us (84%)
  local copies, waits for them, and re-layouts  7.63 us (14%)
  between operations  0.66 us (1%)
    pallas_call x1, Pallas kernels, grouped(): pl.pallas_call(functools.partial(band_kernel, seq_count, piece_count, gro...  45 us
    unnamed x12, local copies, waits for them, and re-layouts  6.86 us

commit v1 on v0

--- a/solution.py
+++ b/solution.py
@@ -106,6 +106,14 @@
             device_id=at(mine, to, piece), device_id_type=MESH,
         )
 
+    def keep(kind, pair):
+        source = (k_ref, v_ref, q_ref, do_ref)[kind]
+        target = (kg, vg, qg, dg)[kind]
+        base = (group, group, 0, 0)[kind]
+        return pltpu.make_async_copy(
+            source.at[:, cols(member, pair)], target.at[pair, block(base + member)], in_s.at[kind, pair, 0]
+        )
+
     def forward(kind, pair, index):
         target = (kg, vg)[kind]
         return pltpu.make_async_remote_copy(
@@ -139,17 +147,16 @@
     def landed(target, sem):
         pltpu.make_async_copy(target, target, sem).wait()
 
-    order = ((0, 1), (2, 3))
-    for kinds in order:
-        for pair in range(pairs):
+    for pair in range(pairs):
+        for kinds in ((0, 1), (2, 3)):
             for step in range(1, group):
                 for kind in kinds:
                     spread(kind, pair, step).start()
             for kind in kinds:
-                source = (k_ref, v_ref, q_ref, do_ref)[kind]
-                base = (group, group, 0, 0)[kind]
-                (kg, vg, qg, dg)[kind][pair, block(base + member), :] = source[:, cols(member, pair)]
+                keep(kind, pair).start()
             if kinds == (0, 1):
+                for kind in kinds:
+                    keep(kind, pair).wait()
 
                 @pl.when(has_next)
                 def _(pair=pair):
@@ -174,16 +181,6 @@
     en[...] = dot(emb_ref[...], twice.astype(jnp.bfloat16)).astype(jnp.bfloat16)
     det[...] = jnp.zeros_like(det)
 
-    for pair in range(pairs):
-        for step in range(1, group):
-            for kind in (0, 1):
-                spread(kind, pair, step).wait_recv()
-
-            @pl.when(has_next)
-            def _(pair=pair, step=step):
-                for kind in (0, 1):
-                    forward(kind, pair, lax.rem(member + group - step, group)).start()
-
     scale = HEAD_DIM ** (-0.5)
     lane = lax.broadcasted_iota(jnp.int32, (1, LANES), 1)
     low = (lane < HEAD_DIM).astype(jnp.float32)
@@ -194,9 +191,22 @@
             [value * (low * factor).astype(jnp.bfloat16), value * (high * factor).astype(jnp.bfloat16)], axis=0
         )
 
+    def pass_on(pair, step):
+        for kind in (0, 1):
+            spread(kind, pair, step).wait_recv()
+
+        @pl.when(has_next)
+        def _():
+            for kind in (0, 1):
+                forward(kind, pair, lax.rem(member + group - step, group)).start()
+
+    for step in range(1, group):
+        pass_on(0, step)
+
     for pair in range(pairs):
-        for step in range(1, group):
-            for kind in (2, 3):
+        for kind in (2, 3):
+            keep(kind, pair).wait()
+            for step in range(1, group):
                 spread(kind, pair, step).wait_recv()
 
         @pl.when(has_prev)
@@ -209,6 +219,12 @@
         dvt[...] = jnp.zeros_like(dvt)
 
         def step_block(index, carry, pair=pair):
+            if pair < pairs - 1:
+
+                @pl.when(index > 0)
+                def _():
+                    pass_on(pair + 1, index)
+
             start = pl.multiple_of(index * rows, rows)
             span = pl.ds(start, window)
             q2 = halves(qg[pair, pl.ds(start, rows), :], scale)
@@ -302,13 +318,6 @@
     for step in range(1, groups):
         across(step).start()
 
-    for pair in range(pairs):
-        for step in range(1, group):
-            source = lax.rem(member + step, group)
-            landed(ql.at[source, pair], q_r.at[pair, source])
-        for index in range(group):
-            gq_ref[:, (index * pairs + pair) * LANES : (index * pairs + pair + 1) * LANES] = ql[index, pair]
-
     for step in range(1, groups):
         across(step).wait_recv()
     total = l2[0]
@@ -318,6 +327,13 @@
     de_all[own_rows, :] = total
     for step in range(1, mates):
         give(step).start()
+
+    for pair in range(pairs):
+        for step in range(1, group):
+            source = lax.rem(member + step, group)
+            landed(ql.at[source, pair], q_r.at[pair, source])
+        for index in range(group):
+            gq_ref[:, (index * pairs + pair) * LANES : (index * pairs + pair + 1) * LANES] = ql[index, pair]
 
     for pair in range(pairs):
         for step in range(1, group):
@@ -400,7 +416,7 @@
     return pl.pallas_call(
         functools.partial(band_kernel, seq_count, piece_count, group, pairs),
         out_shape=(out, out, out, jax.ShapeDtypeStruct((BAND_EXTENT, HEAD_DIM), f32)),
-        in_specs=[whole] * 5,
+        in_specs=[pl.BlockSpec(memory_space=pltpu.HBM)] * 4 + [whole],
         out_specs=(whole,) * 4,
         scratch_shapes=[
             vmem((pairs, group * rows, LANES), b16), vmem((pairs, group * rows, LANES), b16),

time: 53.5 us -> 52 us (0.972)
  Pallas kernels: 45 us -> 43.4 us
    pallas_call x1, Pallas kernels: 45 us -> 43.4 us  [grouped(): pl.pallas_call(functools.partial(band_kernel, seq_count, piece_count, gro...]
where the time goes in v1:
time: 52 us; the launch traced here: 51.7 us
  Pallas kernels  43.4 us (83%)
  local copies, waits for them, and re-layouts  7.63 us (15%)
  between operations  0.66 us (1%)
    pallas_call x1, Pallas kernels, grouped(): pl.pallas_call(functools.partial(band_kernel, seq_count, piece_count, gro...  43.4 us
    unnamed x12, local copies, waits for them, and re-layouts  6.86 us

profile of v1, /device:TPU:0, one launch (start us, length us, event | category | flops | bytes accessed | tf_op | source)
XLA Modules:
  0.0 51.7 jit_solution(15374963114379092551)
XLA Ops:
  0.6 1.0 %copy.9.emb_ref = bf16[512,64]{1,0:T(8,128)(2,1)S(1)} copy(bf16[512,64]{0,1:T(8,128)(2,1)} %param.9) | data formatting | bytes 131072 | tf_op args[4]
  1.6 0.0 copy-start
  1.6 0.9 %copy-done = bf16[128,1024]{1,0:T(8,128)(2,1)S(1)} copy-done((bf16[128,1024]{1,0:T(8,128)(2,1)S(1)}, bf16[128,1024]{1,0:T(8,128)(2,1)}, u32[]{:S(2)}) %copy-start) | copy-done | bytes 262168
  2.5 0.0 copy-start.1
  2.6 0.9 %copy-done.1 = bf16[128,1024]{1,0:T(8,128)(2,1)S(1)} copy-done((bf16[128,1024]{1,0:T(8,128)(2,1)S(1)}, bf16[128,1024]{1,0:T(8,128)(2,1)}, u32[]{:S(2)}) %copy-start.1) | copy-done | bytes 262168
  3.5 0.0 copy-start.2
  3.5 0.9 %copy-done.2 = bf16[128,1024]{1,0:T(8,128)(2,1)S(1)} copy-done((bf16[128,1024]{1,0:T(8,128)(2,1)S(1)}, bf16[128,1024]{1,0:T(8,128)(2,1)}, u32[]{:S(2)}) %copy-start.2) | copy-done | bytes 262168
  4.5 0.0 copy-start.3
  4.5 0.9 %copy-done.3 = bf16[128,1024]{1,0:T(8,128)(2,1)S(1)} copy-done((bf16[128,1024]{1,0:T(8,128)(2,1)S(1)}, bf16[128,1024]{1,0:T(8,128)(2,1)}, u32[]{:S(2)}) %copy-start.3) | copy-done | bytes 262168
  5.4 43.4 %shard_map.84 = (bf16[128,1024]{1,0:T(8,128)(2,1)S(1)}, bf16[128,1024]{1,0:T(8,128)(2,1)S(1)}, bf16[128,1024]{1,0:T(8,128)(2,1)S(1)}, f32[512,64]{1,0:T(8,128)S(1)}) custom-call(bf16[128,1024]{1,0:T(8,128)(2,1)S(1)} %copy-done, bf16[128,1024]{1,0:T(8,128)(2,1)S(1)} %copy-done.1, bf16[128,1024]{1,0:T(8,128)(2,1)S(1)} %copy-done.2, ...), custom_call_target="tpu_custom_call" | custom-call | tf_op jit(solution)/shard_map/pallas_call | solution.py:416
  48.8 0.8 %copy.10 = f32[512,64]{0,1:T(8,128)} copy(f32[512,64]{1,0:T(8,128)S(1)} %get-tuple-element.7) | data formatting | bytes 262144 | tf_op jit(solution)/shard_map/pallas_call | solution.py:416
  49.6 0.7 %copy.14 = bf16[128,1024]{1,0:T(8,128)(2,1)} copy(bf16[128,1024]{1,0:T(8,128)(2,1)S(1)} %get-tuple-element.12) | data formatting | bytes 524288
  50.3 0.7 %copy.15 = bf16[128,1024]{1,0:T(8,128)(2,1)} copy(bf16[128,1024]{1,0:T(8,128)(2,1)S(1)} %get-tuple-element.13) | data formatting | bytes 524288
  51.0 0.7 %copy.16 = bf16[128,1024]{1,0:T(8,128)(2,1)} copy(bf16[128,1024]{1,0:T(8,128)(2,1)S(1)} %get-tuple-element.14) | data formatting | bytes 524288
Async XLA Ops:
  1.6 1.0 %copy-start = (bf16[128,1024]{1,0:T(8,128)(2,1)S(1)}, bf16[128,1024]{1,0:T(8,128)(2,1)}, u32[]{:S(2)}) copy-start(bf16[128,1024]{1,0:T(8,128)(2,1)} %q_ref.1) | copy-start | bytes 786436
  2.5 0.9 %copy-start.1 = (bf16[128,1024]{1,0:T(8,128)(2,1)S(1)}, bf16[128,1024]{1,0:T(8,128)(2,1)}, u32[]{:S(2)}) copy-start(bf16[128,1024]{1,0:T(8,128)(2,1)} %k_ref.1) | copy-start | bytes 786436
  3.5 0.9 %copy-start.2 = (bf16[128,1024]{1,0:T(8,128)(2,1)S(1)}, bf16[128,1024]{1,0:T(8,128)(2,1)}, u32[]{:S(2)}) copy-start(bf16[128,1024]{1,0:T(8,128)(2,1)} %v_ref.1) | copy-start | bytes 786436
  4.5 0.9 %copy-start.3 = (bf16[128,1024]{1,0:T(8,128)(2,1)S(1)}, bf16[128,1024]{1,0:T(8,128)(2,1)}, u32[]{:S(2)}) copy-start(bf16[128,1024]{1,0:T(8,128)(2,1)} %do_ref.1) | copy-start | bytes 786436
